TPU v7x, 128 devices: a whole 4x4x4 slice. The times are simulated.
128 devices in a mesh: dp: 128 (over y, z, x, core).
Axes of the slice: x: 4, y: 4, z: 4, core: 2. Of those that a mesh axis runs over, the one named last changes fastest.
Arguments:
- buffer_small: bfloat16 [2048, 8, 8, 640], P('dp'), may hold values from -6 to 6
- buffer_large: bfloat16 [1024, 12, 12, 640], P('dp'), may hold values from -6 to 6
- fetch_small: int32 [256], P('dp'), may hold values from 0 to 15, as said below
- fetch_large: int32 [128], P('dp'), may hold values from 0 to 7, as said below
- reinit_small: int32 [256], P('dp'), may hold values 0 or 1
- reinit_large: int32 [128], P('dp'), may hold values 0 or 1
- fresh_small: bfloat16 [256, 8, 8, 640], P('dp'), may hold values from -1 to 1
- fresh_large: bfloat16 [128, 12, 12, 640], P('dp'), may hold values from -1 to 1
- noise_small: bfloat16 [2, 256, 8, 8, 640], P(None, 'dp'), may hold values from -2 to 2
- noise_large: bfloat16 [2, 128, 12, 12, 640], P(None, 'dp'), may hold values from -2 to 2
- probe_small: bfloat16 [256, 8, 8, 640], P('dp'), may hold values from -6 to 6
- probe_large: bfloat16 [128, 12, 12, 640], P('dp'), may hold values from -6 to 6
- train_maps: bfloat16 [512, 12, 12, 640], P('dp'), may hold values from -6 to 6
- train_group: int32 [512], P('dp'), may hold values 0 or 1
- train_cot: bfloat16 [512, 12, 12, 640], P('dp'), may hold values from -6 to 6
- kernel_one: bfloat16 [3, 3, 640, 640], replicated, may hold values from -0.078125 to 0.078125
- bias_one: float32 [640], replicated, may hold values from -3 to 3
- kernel_two: bfloat16 [3, 3, 640, 640], replicated, may hold values from -0.078125 to 0.078125
- bias_two: float32 [640], replicated, may hold values from -3 to 3
Outputs:
- samples_small: bfloat16 [256, 8, 8, 640], P('dp')
- samples_large: bfloat16 [128, 12, 12, 640], P('dp')
- buffer_small_new: bfloat16 [2048, 8, 8, 640], P('dp')
- buffer_large_new: bfloat16 [1024, 12, 12, 640], P('dp')
- train_out: bfloat16 [512, 12, 12, 640], P('dp')
- train_grad: float32 [512, 12, 12, 640], P('dp')
- grad_kernel_one: float32 [3, 3, 640, 640], replicated
- grad_bias_one: float32 [640], replicated
- grad_kernel_two: float32 [3, 3, 640, 640], replicated
- grad_bias_two: float32 [640], replicated
Inputs may be any that keep to these rules, and one draw needn't show every extreme that they name: `fetch_small`: within each aligned block of 2 entries that starts at a multiple of 2, the numbers are distinct. `fetch_large`: within each aligned block of 1 entries that starts at a multiple of 1, the numbers are distinct.
All inputs are finite; a program needn't handle non-finite values. No bound on the sum of `reinit_small` or of `reinit_large` or of `train_group` on one device may be relied on, other than what follows from the above.
Results may differ from a plain program's by a relative error of at most 0.0057.
Values may be sent and summed in bfloat16 or wider, within the bound.
A program may use at most 256 MiB of HBM per device.

v0:
```python
import functools

import jax
import jax.numpy as jnp
from jax import lax
from jax.experimental import pallas as pl
from jax.experimental.pallas import tpu as pltpu
from jax.sharding import PartitionSpec as P

MESH = pl.DeviceIdType.MESH
F32 = jnp.float32
BF16 = jnp.bfloat16
STRIDES = (2, 8, 32)
KINDS = 48
SMALL_HOPS = (21, 64)
LARGE_HOP = 106


class Place:
    def __init__(self):
        me = lax.axis_index("dp")
        self.me = me
        self.core = lax.rem(me, 2)
        self.sib = me + 1 - 2 * self.core
        self.coord = [lax.rem(me // s, 4) for s in STRIDES]

    def near(self, axis, step):
        m = self.coord[axis]
        return self.me + (lax.rem(m + step, 4) - m) * STRIDES[axis]

    def hop(self, steps):
        return lax.rem(self.me + steps, 128)


class Copy:
    def __init__(self, src, dst, send, recv, dev):
        self.fields = dict(src_ref=src, dst_ref=dst, send_sem=send, recv_sem=recv, device_id=(dev,), device_id_type=MESH)

    def start(self):
        pltpu.make_async_remote_copy(**self.fields).start()

    def wait_send(self):
        pltpu.make_async_remote_copy(**self.fields).wait_send()

    def wait_recv(self):
        pltpu.make_async_remote_copy(**self.fields).wait_recv()


def rows_loop(total, step, body):
    def run(i, carry):
        body(pl.multiple_of(i * step, step))
        return carry

    lax.fori_loop(0, total // step, run, 0)


def peers(place):
    near = [place.near(a, s) for a in range(3) for s in (1, 2, 3)] + [place.sib]
    return near + [place.hop(s) for s in (21, 107, 64, 106, 22)]


def arrive(place):
    for device in peers(place):
        pl.semaphore_signal(pltpu.get_barrier_semaphore(), inc=1, device_id=(device,), device_id_type=MESH)


def all_arrived(place):
    pl.semaphore_wait(pltpu.get_barrier_semaphore(), len(peers(place)))


def sigmoid(v):
    return 1.0 / (1.0 + jnp.exp(-v))


def silu_slope(v):
    s = sigmoid(v)
    return s * (1.0 + v * (1.0 - s))


def rounded(v):
    return v.astype(BF16).astype(F32)


def dot(a, b):
    return jnp.dot(a, b, preferred_element_type=F32)


def dot_nt(a, b):
    return lax.dot_general(a, b, (((1,), (1,)), ((), ())), preferred_element_type=F32)


class Reduce:
    def __init__(self, refs):
        self.__dict__.update(refs)
        self.kinds = {}
        self.steps = (
            self.c0, self.s1, self.s1b, self.s2, self.s3, self.t3, self.t2, self.t1, self.t1b, self.t1c, self.t0,
            self.left, self.left_last, self.b0, self.b1,
        )

    def axes(self, p):
        return [p, (p + 1) % 3, (p + 2) % 3]

    def copy(self, c, p, kind, src, dst, dev):
        k = self.kinds.setdefault(kind, len(self.kinds))
        return Copy(src, dst, self.sends.at[c, p, k], self.recvs.at[c, p, k], dev)

    def span(self, core, block, start, size):
        return pl.ds(pl.multiple_of(core * 960 + block * 240 + start, 16), size)

    def d0(self, c, p):
        P = self.place
        far = pl.ds(pl.multiple_of((1 - P.core) * 960, 16), 960)
        return self.copy(c, p, "core", self.g.at[c, p, far], self.sib.at[c, p], P.sib)

    def d1(self, c, p):
        P = self.place
        ax = self.axes(p)[0]
        m = P.coord[ax]
        right, left, across = [lax.rem(m + d, 4) for d in (1, 3, 2)]
        dr, dl = P.near(ax, 1), P.near(ax, 3)
        first = lambda b: self.sib.at[c, p, self.span(0, b, 0, 128)]
        second = lambda b: self.sib.at[c, p, self.span(0, b, 128, 112)]
        h0, h1 = pl.ds(0, 128), pl.ds(128, 112)
        return dict(
            ar=self.copy(c, p, "1ar", first(across), self.r1o.at[c, p, 0], dr),
            al=self.copy(c, p, "1al", second(across), self.r1o.at[c, p, 1, pl.ds(0, 112)], dl),
            ra=self.copy(c, p, "1ra", second(right), self.r1.at[c, p, 0, h1], dr),
            la=self.copy(c, p, "1la", first(left), self.r1.at[c, p, 1, h0], dl),
            rb=self.copy(c, p, "1rb", first(right), self.r1.at[c, p, 0, h0], dr),
            lb=self.copy(c, p, "1lb", second(left), self.r1.at[c, p, 1, h1], dl),
        )

    def d2(self, c, p):
        P = self.place
        ax = self.axes(p)[1]
        return [
            self.copy(c, p, "2" + str(s), self.q1.at[c, p, lax.rem(P.coord[ax] + s, 4)], self.r2.at[c, p, s - 1], P.near(ax, s))
            for s in (2, 1, 3)
        ]

    def d3(self, c, p):
        P = self.place
        ax = self.axes(p)[2]
        return [
            self.copy(c, p, "3" + str(s), self.q2.at[c, p, lax.rem(P.coord[ax] + s, 4)], self.r3.at[c, p, s - 1], P.near(ax, s))
            for s in (2, 1, 3)
        ]

    def piece(self, p):
        second, third = self.axes(p)[1:]
        return pl.ds(pl.multiple_of(self.place.coord[second] * 64 + self.place.coord[third] * 16, 16), 16)

    def e3(self, c, p):
        third = self.axes(p)[2]
        mine = self.a2.at[c, p, self.piece(p)]
        return [self.copy(c, p, "e3" + str(s), mine, mine, self.place.near(third, s)) for s in (2, 1, 3)]

    def e2(self, c, p):
        second = self.axes(p)[1]
        mine = self.a2.at[c, p, pl.ds(pl.multiple_of(self.place.coord[second] * 64, 16), 64)]
        return [self.copy(c, p, "e2" + str(s), mine, mine, self.place.near(second, s)) for s in (2, 1, 3)]

    def e1(self, c, p):
        P = self.place
        ax = self.axes(p)[0]
        m = P.coord[ax]
        dr, dl = P.near(ax, 1), P.near(ax, 3)
        right, left, across = [lax.rem(m + d, 4) for d in (1, 3, 2)]
        block = lambda b: self.g.at[c, p, self.span(P.core, b, 0, 240)]
        first = lambda b: self.g.at[c, p, self.span(P.core, b, 0, 128)]
        second = lambda b: self.g.at[c, p, self.span(P.core, b, 128, 112)]
        src = self.a2.at[c, p, pl.ds(0, 240)]
        cp = functools.partial(self.copy, c, p)
        return dict(
            r=cp("e1r", src, block(m), dr),
            l=cp("e1l", src, block(m), dl),
            s=cp("e1s", src, block(m), P.sib),
            fr=cp("e1fr", first(left), first(left), dr),
            fl=cp("e1fl", second(right), second(right), dl),
            sr=cp("e1sr", block(right), block(right), P.sib),
            sl=cp("e1sl", block(left), block(left), P.sib),
            s0=cp("e1s0", first(across), first(across), P.sib),
            s1=cp("e1s1", second(across), second(across), P.sib),
        )

    def own(self, c, p):
        m = self.place.coord[self.axes(p)[0]]
        src = self.a2.at[c, p, pl.ds(0, 240)]
        return pltpu.make_async_copy(src, self.g.at[c, p, self.span(self.place.core, m, 0, 240)], self.local.at[c, p])

    def c0(self, c, p):
        self.d0(c, p).start()

    def s1(self, c, p):
        self.d0(c, p).wait_send()
        pl.semaphore_signal(self.free.at[c, p], inc=1, device_id=(self.place.sib,), device_id_type=MESH)
        self.d0(c, p).wait_recv()

        def add(r0):
            rows = pl.ds(r0, 48)
            mine = pl.ds(pl.multiple_of(self.place.core * 960 + r0, 16), 48)
            self.sib[c, p, rows, :] = (self.sib[c, p, rows, :].astype(F32) + self.g[c, p, mine, :].astype(F32)).astype(BF16)

        rows_loop(960, 48, add)
        d = self.d1(c, p)
        for k in ("ar", "al", "ra", "la"):
            d[k].start()

    def s1b(self, c, p):
        d = self.d1(c, p)
        m = self.place.coord[self.axes(p)[0]]
        right, left = lax.rem(m + 1, 4), lax.rem(m + 3, 4)

        def add(block, start, count, slot):
            def some(r0):
                to = pl.ds(pl.multiple_of(block * 240 + start + r0, 16), 16)
                part = self.r1o[c, p, slot, pl.ds(r0, 16), :].astype(F32)
                self.sib[c, p, to, :] = (self.sib[c, p, to, :].astype(F32) + part).astype(BF16)

            rows_loop(count, 16, some)

        d["ar"].wait_recv()
        add(right, 0, 128, 0)
        d["rb"].start()
        d["al"].wait_recv()
        add(left, 128, 112, 1)
        d["lb"].start()

    def s2(self, c, p):
        d = self.d1(c, p)
        m = self.place.coord[self.axes(p)[0]]
        for k in ("ra", "la", "rb", "lb"):
            d[k].wait_recv()

        def add(r0):
            rows = pl.ds(r0, 16)
            mine = pl.ds(pl.multiple_of(m * 240 + r0, 16), 16)
            total = self.sib[c, p, mine, :].astype(F32) + self.r1[c, p, 0, rows, :].astype(F32)
            total = total + self.r1[c, p, 1, rows, :].astype(F32)
            b = r0 // 64
            self.q1[c, p, b, pl.ds(pl.multiple_of(r0 - b * 64, 16), 16), :] = total.astype(BF16)

        rows_loop(240, 16, add)
        self.q1[c, p, 3, 48:64, :] = jnp.zeros((16, 640), BF16)
        for k in self.d2(c, p):
            k.start()

    def level2(self, c, p, b):
        m = self.place.coord[self.axes(p)[1]]
        rows = pl.ds(pl.multiple_of(b * 16, 16), 16)
        total = self.q1[c, p, m, rows, :].astype(F32)
        for s in range(3):
            total = total + self.r2[c, p, s, rows, :].astype(F32)
        return total

    def s3(self, c, p):
        for k in self.d2(c, p):
            k.wait_recv()

        def add(b, carry):
            self.q2[c, p, b] = self.level2(c, p, b).astype(BF16)
            return carry

        lax.fori_loop(0, 4, add, 0)
        for k in self.d3(c, p):
            k.start()

    def t3(self, c, p):
        for k in self.d3(c, p):
            k.wait_recv()
        total = self.level2(c, p, self.place.coord[self.axes(p)[2]])
        for s in range(3):
            total = total + self.r3[c, p, s].astype(F32)
        self.a2[c, p, self.piece(p), :] = total.astype(BF16)
        for k in self.e3(c, p):
            k.start()

    def t2(self, c, p):
        for k in self.e3(c, p):
            k.wait_recv()
        for k in self.e2(c, p):
            k.start()

    def t1(self, c, p):
        for k in self.e2(c, p):
            k.wait_recv()
        e = self.e1(c, p)
        e["r"].start()
        e["l"].start()
        pl.semaphore_wait(self.free.at[c, p], 1)
        e["s"].start()
        self.own(c, p).start()

    def t1b(self, c, p):
        e = self.e1(c, p)
        e["r"].wait_recv()
        e["fr"].start()
        e["sl"].start()
        e["l"].wait_recv()
        e["fl"].start()
        e["sr"].start()

    def t1c(self, c, p):
        e = self.e1(c, p)
        e["fr"].wait_recv()
        e["s0"].start()
        e["fl"].wait_recv()
        e["s1"].start()

    def t0(self, c, p):
        e = self.e1(c, p)
        for k in ("s", "sr", "sl", "s0", "s1"):
            e[k].wait_recv()
        self.own(c, p).wait()

    def bias_copies(self, level):
        P = self.place
        if level == 0:
            peers = [(0, P.sib, P.core)]
        else:
            peers = [(s, P.near(level - 1, s), P.coord[level - 1]) for s in (1, 2, 3)]
        return [
            self.copy(0, 0, "b%d%d" % (level, s), self.bias.at[level, slot], self.bias.at[level, slot], dev)
            for s, dev, slot in peers
        ]

    def b0(self, c, p):
        level = 3 * c + p
        for k in self.bias_copies(level):
            k.start()

    def b1(self, c, p):
        level = 3 * c + p
        for k in self.bias_copies(level):
            k.wait_recv()
        total = self.bias[level, 0] + self.bias[level, 1]
        if level:
            total = total + self.bias[level, 2] + self.bias[level, 3]
        if level < 3:
            self.bias[level + 1, self.place.coord[level]] = total
            self.b0((level + 1) // 3, (level + 1) % 3)
        else:
            self.bias_out[...] = total

    def left(self, c, p):
        for k in list(self.d1(c, p).values()) + self.d2(c, p) + self.d3(c, p) + self.e3(c, p) + self.e2(c, p):
            k.wait_send()

    def left_last(self, c, p):
        for k in self.e1(c, p).values():
            k.wait_send()

    def finish(self):
        for p in range(3):
            self.left_last(1, p)
        for level in range(4):
            for k in self.bias_copies(level):
                k.wait_send()


def reduce_scratch():
    v = lambda *s: pltpu.VMEM((2, 3) + s, BF16)
    sems = pltpu.SemaphoreType.DMA((2, 3, KINDS))
    return dict(
        sib=v(960, 640),
        r1=v(2, 240, 640),
        r1o=v(2, 128, 640),
        r2=v(3, 64, 640),
        r3=v(3, 16, 640),
        q1=v(4, 64, 640),
        q2=v(4, 16, 640),
        a2=v(256, 640),
        bias=pltpu.VMEM((4, 4, 8, 640), F32),
        sends=sems,
        recvs=sems,
        local=pltpu.SemaphoreType.DMA((2, 3)),
        free=pltpu.SemaphoreType.REGULAR((2, 3)),
    )


class Block:
    def __init__(self, refs):
        self.__dict__.update(refs)

    def load(self, which, r):
        src = (self.kernel_one, self.kernel_two)[which].at[r]
        return pltpu.make_async_copy(src, self.taps.at[r], self.tap_sems.at[r])

    def wait_taps(self, r):
        self.load(0, r).wait()

    def fetch(self, name):
        k = self.inputs.index(name)
        return pltpu.make_async_copy(getattr(self, name), getattr(self, name + "_v"), self.in_sems.at[k])

    def begin(self):
        zeros = jnp.zeros((16, 640), F32)
        self.borders()
        self.xp[0:8, :] = zeros[:8]
        self.xp[584:592, :] = zeros[:8]
        for start in (0, 80, 160):
            self.xs[start : start + 16, :] = zeros[:16]
        self.xl[0:16, :] = zeros[:16]
        self.xl[160:176, :] = zeros[:16]

        def edges(base, count, column):
            n = lax.broadcasted_iota(jnp.int32, (count, 128), 0)
            j, last = column(n)
            self.edge[0, base : base + count, :] = jnp.where(j > 0, 1.0, 0.0)
            self.edge[1, base : base + count, :] = jnp.where(j < last, 1.0, 0.0)

        def twelfth(n):
            return (n * 43691) >> 19

        def wide(n):
            return n - 12 * twelfth(n), 11

        edges(0, 576, lambda n: wide(n >> 2))
        edges(576, 128, lambda n: (n & 7, 7))
        edges(704, 144, wide)
        n = lax.broadcasted_iota(jnp.int32, (576, 128), 0)
        cell = n >> 2
        i = twelfth(cell)
        j = cell - 12 * i
        keep = jnp.where((i < 8) & (j < 8), 1.0, 0.0)
        for m in range(4):
            group = jnp.where(self.group[m] == 1, 1.0, 0.0)
            keep = jnp.maximum(keep, jnp.where((n & 3) == m, group, 0.0))
        self.region[...] = keep

    def borders(self):
        self.cols[0:48, :] = jnp.zeros((48, 1920), BF16)
        self.cols[624:672, :] = jnp.zeros((48, 1920), BF16)

    def train_cols(self, sign):
        for q in range(3):
            dj = sign * (q - 1)
            v = self.xp[pl.ds(8 + dj * 4, 576), :]
            if dj:
                v = v * self.edge[(dj + 1) // 2, 0:576, 0:1]
            self.cols[48:624, q * 640 : (q + 1) * 640] = v.astype(BF16)

    def chain_cols(self, sign):
        for r in range(3):
            self.chain_row(r, sign, self.cols.at[pl.ds(272 * r, 272)])

    def chain_row(self, r, sign, cols):
        for q in range(3):
            dj = sign * (q - 1)
            to = pl.ds(q * 640, 640)
            for m in range(2):
                v = self.xs[pl.ds(16 + 80 * m + sign * (r - 1) * 8 + dj, 64), :]
                if dj:
                    v = v * self.edge[(dj + 1) // 2, 576 + 64 * m : 640 + 64 * m, 0:1]
                cols[64 * m : 64 * m + 64, to] = v.astype(BF16)
            v = self.xl[pl.ds(16 + sign * (r - 1) * 12 + dj, 144), :]
            if dj:
                v = v * self.edge[(dj + 1) // 2, 704:848, 0:1]
            cols[128:272, to] = v.astype(BF16)

    def clear(self):
        self.acc[...] = jnp.zeros((576, 640), F32)

    def product(self, r, rows, back, cols):
        taps = self.taps.at[r]
        if back:
            total = None
            for q in range(3):
                cut = pl.ds(q * 640, 640)
                part = dot_nt(cols[:, cut], taps[cut, :])
                total = part if total is None else total + part
        else:
            total = dot(cols[...], taps[...])
        self.acc[0:rows, :] += total

    def train_side(self, r, sign):
        return self.cols.at[pl.ds(pl.multiple_of(48 + sign * (r - 1) * 48, 16), 576)]

    def train_conv(self, back, wait, then, r):
        if wait:
            self.wait_taps(r)
        self.product(r, 576, back, self.train_side(r, -1 if back else 1))
        if then is not None:
            self.load(then, r).start()

    def chain_conv(self, back, wait, then, r):
        if wait is not None:

            @pl.when(wait)
            def _():
                self.wait_taps(r)

        self.product(r, 272, back, self.cols.at[pl.ds(pl.multiple_of(272 * r, 16), 272)])
        if then is not None:
            self.load(then, r).start()

    def train_wgrad(self, chunk, r):
        side = self.train_side(r, -1)
        for start, size in ((0, 768), (768, 768), (1536, 384)):
            part = dot(self.turned[...], side[:, start : start + size]).astype(BF16)
            for q in range(3):
                low, high = max(start, q * 640), min(start + size, q * 640 + 640)
                if low < high:
                    self.g[chunk, r, q * 640 : q * 640 + 640, low - q * 640 : high - q * 640] = part[:, low - start : high - start]

    def map_rows(self, ref, r0):
        return ref[pl.ds(r0 // 4, 12)].astype(F32).reshape(48, 640)

    def train_start(self):
        self.fetch("maps").wait()
        def some(r0):
            rows = pl.ds(r0, 48)
            v = self.map_rows(self.maps_v, r0)
            a = (v * sigmoid(v) * self.region[rows, 0:1]).astype(BF16)
            self.low_in[rows, :] = a
            self.xp[pl.ds(pl.multiple_of(r0 + 8, 8), 48), :] = a.astype(F32)

        rows_loop(576, 48, some)
        self.train_cols(1)
        self.clear()

    def train_middle(self):
        self.fetch("cot").wait()
        self.sums[...] = jnp.zeros((8, 640), F32)

        def some(r0):
            rows = pl.ds(r0, 48)
            v = self.acc[rows, :] + self.bias_one[...].reshape(1, 640)
            keep = self.region[rows, 0:1]
            self.low_mid[rows, :] = (v * sigmoid(v) * keep).astype(BF16)
            self.pre_one[rows, :] = silu_slope(v) * keep
            c = self.map_rows(self.cot_v, r0) * keep
            self.xp[pl.ds(pl.multiple_of(r0 + 8, 8), 48), :] = c
            self.sums[1:2, :] += jnp.sum(c, axis=0, keepdims=True)

        rows_loop(576, 48, some)
        self.turned[...] = self.low_mid[...].T
        self.train_cols(-1)
        self.clear()

    def train_back(self):
        def some(r0):
            rows = pl.ds(r0, 48)
            v = rounded(self.acc[rows, :] * self.pre_one[rows, :])
            self.xp[pl.ds(pl.multiple_of(r0 + 8, 8), 48), :] = v
            self.sums[0:1, :] += jnp.sum(v, axis=0, keepdims=True)

        rows_loop(576, 48, some)
        self.turned[...] = self.low_in[...].T
        self.bias[0, self.place.core] = self.sums[...]
        self.train_cols(-1)

    def put_xp(self, low):
        def some(r0):
            rows = pl.ds(r0, 48)
            self.xp[pl.ds(pl.multiple_of(r0 + 8, 8), 48), :] = low[rows, :].astype(F32)

        rows_loop(576, 48, some)
        self.train_cols(1)
        self.clear()

    def train_grad_end(self):
        def some(r0):
            rows = pl.ds(r0, 48)
            keep = self.region[rows, 0:1]
            slope = silu_slope(self.map_rows(self.maps_v, r0)) * keep
            self.acc[rows, :] = self.map_rows(self.cot_v, r0) * keep + self.acc[rows, :] * slope

        rows_loop(576, 48, some)
        self.grad[...] = self.acc[...].reshape(144, 4, 640)

    def train_out_end(self):
        def some(r0):
            rows = pl.ds(r0, 48)
            v = self.map_rows(self.maps_v, r0) + (self.acc[rows, :] + self.bias_two[...].reshape(1, 640))
            self.acc[rows, :] = v * self.region[rows, 0:1]

        rows_loop(576, 48, some)
        self.out[...] = self.acc[...].astype(BF16).reshape(144, 4, 640)

    def chain_peers(self):
        P = self.place
        pairs = []
        for s in range(2):
            cut = pl.ds(8 * s, 8)
            pairs.append((s, self.chosen_small.at[cut], self.arrived_small.at[cut], self.samples_small.at[cut], self.ret_small.at[cut], SMALL_HOPS[s]))
        pairs.append((2, self.chosen_large, self.arrived_large, self.samples_large, self.ret_large, LARGE_HOP))
        there = [Copy(a, b, self.go_sems.at[0, k], self.go_sems.at[1, k], P.hop(h)) for k, a, b, _, _, h in pairs]
        back = [Copy(a, b, self.go_sems.at[2, k], self.go_sems.at[3, k], P.hop(128 - h)) for k, _, _, a, b, h in pairs]
        return there, back

    def buffers(self):
        return [
            pltpu.make_async_copy(self.buffer_small, self.g.at[1, 0, pl.ds(0, 1024)], self.buffer_sems.at[0]),
            pltpu.make_async_copy(self.buffer_large, self.g.at[1, 1, pl.ds(0, 1152)], self.buffer_sems.at[1]),
        ]

    def chain_send(self):
        all_arrived(self.place)
        for k in self.buffers():
            k.wait()
        n = lax.broadcasted_iota(jnp.int32, (128, 1024), 0)
        at = lax.broadcasted_iota(jnp.int32, (128, 1024), 1)
        start = jnp.where(n < 64, self.fetch_small[0], self.fetch_small[1]) * 64
        pick = jnp.where(at == start + (n & 63), 1.0, 0.0).astype(BF16)
        rows = dot(pick, self.g[1, 0, 0:1024, :]).astype(BF16)
        self.chosen_small[...] = rows.reshape(16, 8, 640)
        n = lax.broadcasted_iota(jnp.int32, (144, 1152), 0)
        at = lax.broadcasted_iota(jnp.int32, (144, 1152), 1)
        pick = jnp.where(at == n * 8 + self.fetch_large[0], 1.0, 0.0).astype(BF16)
        rows = dot(pick, self.g[1, 1, 0:1152, :]).astype(BF16)
        for i in range(12):
            self.chosen_large[i] = rows[12 * i : 12 * i + 12]
        for k in self.chain_peers()[0]:
            k.start()

    def flat_small(self, ref):
        return ref.astype(F32).reshape(128, 640)

    def spread(self, value):
        for m in range(2):

            def small(r0, m=m):
                self.xs[pl.ds(pl.multiple_of(16 + 80 * m + r0, 8), 16), :] = value(pl.multiple_of(64 * m + r0, 16))

            rows_loop(64, 16, small)

        def large(r0):
            self.xl[pl.ds(pl.multiple_of(16 + r0, 8), 16), :] = value(pl.multiple_of(128 + r0, 16))

        rows_loop(144, 16, large)

    def chain_start(self):
        for name in ("probe_small", "probe_large"):
            self.fetch(name).wait()
        self.probe[0:128, :] = self.flat_small(self.probe_small_v[...])
        for i in range(12):
            self.probe[128 + 12 * i : 140 + 12 * i, :] = self.probe_large_v[i].astype(F32)
        self.spread(lambda r0: self.probe[pl.ds(r0, 16), :])
        self.chain_cols(-1)
        self.clear()

    def chain_state(self):
        for name in ("fresh_small", "fresh_large", "noise_small", "noise_large"):
            self.fetch(name).wait()
        for k in self.chain_peers()[0]:
            k.wait_recv()
        for s in range(2):
            fresh = jnp.where(self.reinit_small[s] == 1, 1.0, 0.0)
            cut = slice(8 * s, 8 * s + 8)
            v = self.fresh_small_v[cut].astype(F32) * fresh + self.arrived_small[cut].astype(F32) * (1.0 - fresh)
            self.state[64 * s : 64 * s + 64, :] = v.reshape(64, 640)
        fresh = jnp.where(self.reinit_large[0] == 1, 1.0, 0.0)
        for i in range(12):
            v = self.fresh_large_v[i].astype(F32) * fresh + self.arrived_large[i].astype(F32) * (1.0 - fresh)
            self.state[128 + 12 * i : 140 + 12 * i, :] = v

    def chain_kept(self):
        self.slope_in[...] = self.acc[0:272, :]

    def chain_act(self):
        def value(r0):
            v = self.state[pl.ds(r0, 16), :]
            return rounded(v * sigmoid(v))

        self.spread(value)
        self.chain_cols(1)
        self.clear()

    def chain_mid(self):
        def value(r0):
            rows = pl.ds(r0, 16)
            v = self.acc[rows, :] + self.bias_one[...].reshape(1, 640)
            return rounded(silu_slope(v) * self.slope_in[rows, :])

        self.spread(value)
        self.chain_cols(-1)
        self.clear()

    def chain_step(self, t):
        late = jnp.where(t == 1, 1.0, 0.0)
        early = 1.0 - late

        def small(r0):
            rows = pl.ds(r0, 16)
            v = self.state[rows, :]
            noise = self.noise_small_v[t, pl.ds(r0 // 8, 2)].astype(F32).reshape(16, 640)
            self.state[rows, :] = v + (self.probe[rows, :] + silu_slope(v) * self.acc[rows, :]) + noise

        rows_loop(128, 16, small)

        def large(r0):
            rows = pl.ds(pl.multiple_of(128 + r0, 16), 16)
            v = self.state[rows, :]
            noise = self.noise_large_v[pl.ds(r0, 16)].astype(F32)
            noise = noise[:, 0, :] * early + noise[:, 1, :] * late
            self.state[rows, :] = v + (self.probe[rows, :] + silu_slope(v) * self.acc[rows, :]) + noise

        rows_loop(144, 16, large)

    def chain_end(self):
        self.samples_small[...] = self.state[0:128, :].astype(BF16).reshape(16, 8, 640)
        for i in range(12):
            self.samples_large[i] = self.state[128 + 12 * i : 140 + 12 * i, :].astype(BF16)
        for k in self.chain_peers()[1]:
            k.start()
        self.borders()
        self.train_cols(-1)
        self.clear()

    def finish(self):
        there, back = self.chain_peers()
        for k in back:
            k.wait_recv()
        for k in there + back:
            k.wait_send()


INPUTS = (
    "maps", "cot", "probe_small", "probe_large", "fresh_small", "fresh_large", "noise_small", "noise_large",
)
OUTPUTS = ("samples_small", "samples_large", "out", "grad")
INPUT_SHAPES = (
    (144, 4, 640), (144, 4, 640), (16, 8, 640), (12, 12, 640), (16, 8, 640), (12, 12, 640), (2, 16, 8, 640), (144, 2, 640),
)


def block_scratch():
    f = lambda *s: pltpu.VMEM(s, F32)
    b = lambda *s: pltpu.VMEM(s, BF16)
    dma = pltpu.SemaphoreType.DMA
    found = {name + "_v": b(*shape) for name, shape in zip(INPUTS, INPUT_SHAPES)}
    found.update(
        taps=b(3, 1920, 640),
        cols=b(816, 1920),
        xp=f(592, 640),
        xs=f(176, 640),
        xl=f(176, 640),
        acc=f(576, 640),
        pre_one=f(576, 640),
        low_in=b(576, 640),
        low_mid=b(576, 640),
        turned=b(640, 576),
        edge=f(2, 848, 128),
        region=f(576, 128),
        sums=f(8, 640),
        probe=f(272, 640),
        state=f(272, 640),
        slope_in=f(272, 640),
        arrived_small=b(16, 8, 640),
        arrived_large=b(12, 12, 640),
        chosen_small=b(16, 8, 640),
        chosen_large=b(12, 12, 640),
        tap_sems=dma((3,)),
        in_sems=dma((len(INPUTS),)),
        buffer_sems=dma((2,)),
        go_sems=dma((4, 3)),
    )
    return found


class Loop:
    def __init__(self, count, body):
        self.count, self.body = count, body


def length(items):
    return sum(i.count * length(i.body(None)) if isinstance(i, Loop) else 1 for i in items)


def schedule(block):
    part = functools.partial

    def conv(back, wait=False, then=None):
        return Loop(3, lambda r: [part(block.train_conv, back, wait, then, r)])

    def chain(back, wait=None, then=None):
        return Loop(3, lambda r: [part(block.chain_conv, back, wait, then, r)])

    def wgrad(chunk):
        return Loop(3, lambda r: [part(block.train_wgrad, chunk, r)])

    def chain_turn(t):
        first = None if t is None else t == 0
        return [block.chain_act, chain(False, wait=first), block.chain_mid, chain(True), part(block.chain_step, t)]

    return [
        block.train_start,
        conv(False, wait=True, then=1),
        block.chain_send,
        block.train_middle,
        wgrad(0),
        conv(True, wait=True),
        block.train_back,
        wgrad(1),
        block.chain_start,
        chain(True, then=0),
        block.chain_kept,
        block.chain_state,
        Loop(2, chain_turn),
        block.chain_end,
        conv(True, then=1),
        block.train_grad_end,
        part(block.put_xp, block.low_mid),
        conv(False, wait=True),
        block.train_out_end,
    ]


def play(items, places, tick):
    done = 0
    for item in items:
        if isinstance(item, Loop):
            size = length(item.body(None))

            def turn(i, carry, item=item, size=size, done=done):
                inner = []
                for condition, base in places:
                    for k in range(item.count):
                        now = i == k
                        inner.append((now if condition is None else condition & now, base + done + k * size))
                play(item.body(i), inner, tick)
                return carry

            lax.fori_loop(0, item.count, turn, 0)
            done += item.count * size
        else:
            item()
            for condition, base in places:
                tick(condition, base + done)
            done += 1


TICKS = {
    6: (0,),
    8: (6, 1,),
    9: (2,),
    10: (7,),
    11: (12, 8,),
    12: (78,),
    13: (13, 3,),
    14: (4, 18, 14, 9,),
    15: (5, 19, 10, 84,),
    17: (11, 20,),
    19: (15, 85,),
    21: (16, 25,),
    22: (24,),
    23: (17, 86,),
    24: (26,),
    25: (21, 30, 22,),
    26: (31,),
    27: (32, 23, 87,),
    28: (36,),
    29: (27,),
    30: (28, 38,),
    32: (29, 33,),
    33: (34, 37, 42,),
    34: (35, 39,),
    35: (40,),
    37: (44, 43, 41,),
    39: (45, 46,),
    41: (48, 47,),
    42: (49,),
    45: (50, 51,),
    46: (52, 53, 54,),
    47: (56, 55, 57,),
    48: (62, 58, 60, 59,),
    49: (66, 67, 68, 69, 70, 71, 72, 73, 74, 63, 64, 61, 65,),
}

B_INPUTS = INPUTS + (
    "buffer_small", "buffer_large", "kernel_one", "kernel_two",
    "group", "reinit_small", "reinit_large", "fetch_small", "fetch_large", "bias_one", "bias_two",
)
B_OUTPUTS = ("g",) + OUTPUTS + ("ret_small", "ret_large", "bias_out")


def block_kernel(names, *given):
    refs = dict(zip(names, given))
    refs.update(place=Place(), inputs=INPUTS)
    block, reduce = Block(refs), Reduce(refs)
    arrive(block.place)
    block.fetch("maps").start()
    for r in range(3):
        block.load(0, r).start()
    for k in block.buffers():
        k.start()
    for name in INPUTS[1:]:
        block.fetch(name).start()
    block.begin()

    def tick(condition, n):
        def run():
            for code in TICKS.get(n, ()):
                reduce.steps[code // 6](code // 3 % 2, code % 3)

        if condition is None:
            run()
        elif n in TICKS:
            pl.when(condition)(run)

    play(schedule(block), [(None, 0)], tick)
    block.finish()
    reduce.finish()


ANYWHERE = pl.BlockSpec(memory_space=pl.ANY)
SCALARS = pl.BlockSpec(memory_space=pltpu.SMEM)
INSIDE = pl.BlockSpec(memory_space=pltpu.VMEM)


def run_block(*args):
    scratch = reduce_scratch()
    scratch.update(block_scratch())
    names = B_INPUTS + B_OUTPUTS + tuple(scratch)
    held = [pltpu.with_memory_space_constraint(a, pltpu.HBM) if k < 12 else a for k, a in enumerate(args)]
    return pl.pallas_call(
        functools.partial(block_kernel, names),
        out_shape=(
            pltpu.VMEM((2, 3, 1920, 640), BF16),
            pltpu.VMEM((16, 8, 640), BF16),
            pltpu.VMEM((12, 12, 640), BF16),
            pltpu.VMEM((144, 4, 640), BF16),
            pltpu.VMEM((144, 4, 640), F32),
            pltpu.VMEM((16, 8, 640), BF16),
            pltpu.VMEM((12, 12, 640), BF16),
            pltpu.VMEM((8, 640), F32),
        ),
        in_specs=[ANYWHERE] * 12 + [SCALARS] * 5 + [INSIDE] * 2,
        out_specs=(INSIDE,) * 8,
        scratch_shapes=list(scratch.values()),
        compiler_params=pltpu.CompilerParams(collective_id=0, has_side_effects=True, vmem_limit_bytes=46 * 2**20),
        cost_estimate=pl.CostEstimate(flops=36 * 10**9, bytes_accessed=80 * 2**20, transcendentals=0),
    )(*held)


END_INPUTS = (
    "g", "samples_small_in", "samples_large_in", "out_in", "grad_in", "ret_small", "ret_large", "bias",
    "buffer_small", "buffer_large", "fetch_small", "fetch_large",
)
END_OUTPUTS = (
    "kernel_one", "kernel_two", "samples_small", "samples_large", "out", "grad", "new_small", "new_large", "bias_one", "bias_two",
)
END_SCRATCH = ("wide", "small", "large", "wide_sems", "sems")
PASSED = ("out", "grad", "samples_small", "samples_large")
CUT = 480
SLOTS = 4


def end_kernel(*given):
    r = dict(zip(END_INPUTS + END_OUTPUTS + END_SCRATCH, given))
    sems = r["sems"]
    small = pltpu.make_async_copy(r["buffer_small"], r["small"], sems.at[4])
    large = pltpu.make_async_copy(r["buffer_large"], r["large"], sems.at[5])
    small.start()
    large.start()
    passed = [pltpu.make_async_copy(r[n + "_in"], r[n], sems.at[k]) for k, n in enumerate(PASSED)]
    per_part = 1920 // CUT
    pending = []
    for n in range(6 * per_part):
        c, part, block = n // (3 * per_part), n // per_part % 3, n % per_part
        slot = n % SLOTS
        target = r["kernel_one"] if c else r["kernel_two"]
        copy = pltpu.make_async_copy(
            r["wide"].at[slot], target.at[pl.ds(part * 1920 + block * CUT, CUT)], r["wide_sems"].at[slot]
        )
        if n >= SLOTS:
            pending[n - SLOTS].wait()

        def some(r0):
            rows = pl.ds(pl.multiple_of(block * CUT + r0, 16), 96)
            r["wide"][slot, pl.ds(r0, 96), :] = r["g"][c, part, rows, :].astype(F32)

        rows_loop(CUT, 96, some)
        copy.start()
        pending.append(copy)
        if n == 0:
            for k in passed:
                k.start()
            r["bias_one"][...] = r["bias"][0, :]
            r["bias_two"][...] = r["bias"][1, :]
        if n == per_part:
            small.wait()
            for s in range(2):
                r["small"][r["fetch_small"][s]] = r["ret_small"][8 * s : 8 * s + 8]
            small = pltpu.make_async_copy(r["small"], r["new_small"], sems.at[4])
            small.start()
        if n == 2 * per_part:
            large.wait()
            chosen = lax.broadcasted_iota(jnp.int32, (12, 8, 640), 1) == r["fetch_large"][0]
            for i in range(12):
                cut = slice(12 * i, 12 * i + 12)
                new = jnp.broadcast_to(r["ret_large"][i].astype(F32)[:, None, :], (12, 8, 640))
                r["large"][cut] = jnp.where(chosen, new, r["large"][cut].astype(F32)).astype(BF16)
            large = pltpu.make_async_copy(r["large"], r["new_large"], sems.at[5])
            large.start()
    for k in pending[-SLOTS:] + passed + [small, large]:
        k.wait()


def run_end(*args):
    shape = pltpu.HBM
    held = [pltpu.with_memory_space_constraint(a, pltpu.HBM) if k in (8, 9) else a for k, a in enumerate(args)]
    return pl.pallas_call(
        end_kernel,
        out_shape=(
            shape((5760, 640), F32),
            shape((5760, 640), F32),
            shape((16, 8, 640), BF16),
            shape((12, 12, 640), BF16),
            shape((144, 4, 640), BF16),
            shape((144, 4, 640), F32),
            shape((16, 8, 8, 640), BF16),
            shape((144, 8, 640), BF16),
            jax.ShapeDtypeStruct((640,), F32),
            jax.ShapeDtypeStruct((640,), F32),
        ),
        in_specs=[INSIDE] * 8 + [ANYWHERE] * 2 + [SCALARS] * 2,
        out_specs=(ANYWHERE,) * 8 + (INSIDE,) * 2,
        scratch_shapes=[
            pltpu.VMEM((SLOTS, CUT, 640), F32),
            pltpu.VMEM((16, 8, 8, 640), BF16),
            pltpu.VMEM((144, 8, 640), BF16),
            pltpu.SemaphoreType.DMA((SLOTS,)),
            pltpu.SemaphoreType.DMA((6,)),
        ],
        compiler_params=pltpu.CompilerParams(vmem_limit_bytes=16 * 2**20),
    )(*held)


def map_minor(v):
    return v.transpose(1, 2, 0, 3).reshape(144, v.shape[0], 640)


def map_major(v):
    return v.reshape(12, 12, v.shape[1], 640).transpose(2, 0, 1, 3)


def local(
    buffer_small,
    buffer_large,
    fetch_small,
    fetch_large,
    reinit_small,
    reinit_large,
    fresh_small,
    fresh_large,
    noise_small,
    noise_large,
    probe_small,
    probe_large,
    train_maps,
    train_group,
    train_cot,
    kernel_one,
    bias_one,
    kernel_two,
    bias_two,
):
    g, samples_small, samples_large, out, grad, ret_small, ret_large, bias = run_block(
        map_minor(train_maps),
        map_minor(train_cot),
        probe_small.reshape(16, 8, 640),
        probe_large.reshape(12, 12, 640),
        fresh_small.reshape(16, 8, 640),
        fresh_large.reshape(12, 12, 640),
        noise_small.reshape(2, 16, 8, 640),
        noise_large.transpose(1, 2, 3, 0, 4).reshape(144, 2, 640),
        buffer_small.reshape(1024, 640),
        map_minor(buffer_large).reshape(1152, 640),
        kernel_one.reshape(3, 1920, 640),
        kernel_two.reshape(3, 1920, 640),
        train_group,
        reinit_small,
        reinit_large,
        fetch_small,
        fetch_large,
        bias_one,
        bias_two,
    )
    sums = run_end(
        g, samples_small, samples_large, out, grad, ret_small, ret_large, bias,
        buffer_small, map_minor(buffer_large), fetch_small, fetch_large,
    )
    sum_one, sum_two, samples_small, samples_large, out, grad, new_small, new_large, bias_sum_one, bias_sum_two = sums
    return (
        samples_small.reshape(2, 8, 8, 640),
        samples_large.reshape(1, 12, 12, 640),
        new_small,
        map_major(new_large),
        map_major(out),
        map_major(grad),
        sum_one.reshape(3, 3, 640, 640),
        bias_sum_one,
        sum_two.reshape(3, 3, 640, 640),
        bias_sum_two,
    )


def solution(mesh):
    in_specs = (
        P("dp", None, None, None),
        P("dp", None, None, None),
        P("dp"),
        P("dp"),
        P("dp"),
        P("dp"),
        P("dp", None, None, None),
        P("dp", None, None, None),
        P(None, "dp", None, None, None),
        P(None, "dp", None, None, None),
        P("dp", None, None, None),
        P("dp", None, None, None),
        P("dp", None, None, None),
        P("dp"),
        P("dp", None, None, None),
        P(),
        P(),
        P(),
        P(),
    )
    out_specs = (
        P("dp", None, None, None),
        P("dp", None, None, None),
        P("dp", None, None, None),
        P("dp", None, None, None),
        P("dp", None, None, None),
        P("dp", None, None, None),
        P(),
        P(),
        P(),
        P(),
    )
    return jax.shard_map(local, mesh=mesh, in_specs=in_specs, out_specs=out_specs, check_vma=False)
```

profile of v0, /device:TPU:6, one launch (start us, length us, event | category | flops | bytes accessed | tf_op | source)
XLA Modules:
  0.0 126.8 jit_solution(14468843718441574016)
XLA Ops:
  1.9 0.0 copy-start
  1.9 111.8 %shard_map.258 = (bf16[2,3,1920,640]{3,2,1,0:T(8,128)(2,1)S(1)}, bf16[16,8,640]{2,1,0:T(8,128)(2,1)S(1)}, bf16[12,12,640]{2,1,0:T(8,128)(2,1)S(1)}, bf16[144,4,6...) custom-call(bf16[144,4,640]{2,1,0:T(4,128)(2,1)} %bitcast.44, ...), custom_call_target="tpu_custom_call" | custom-call | flops 35999997952 | bytes 83886080 | tf_op jit(solution)/shard_map/pallas_call | solution.py:918
  113.8 0.0 copy-done
  113.8 12.9 %shard_map.259 = (f32[5760,640]{1,0:T(8,128)}, f32[5760,640]{1,0:T(8,128)}, bf16[16,8,640]{2,1,0:T(8,128)(2,1)}, bf16[12,12,640]{2,1,0:T(8,128)(2,1)}, bf16[144,...) custom-call(bf16[2,3,1920,640]{3,2,1,0:T(8,128)(2,1)S(1)} %get-tuple, ...), custom_call_target="tpu_custom_call" | custom-call | tf_op jit(solution)/shard_map/pallas_call | solution.py:1005
Async XLA Ops:
  1.9 111.8 %copy-start = (s32[2]{0:T(128)S(1)}, s32[2]{0:T(128)}, u32[]{:S(2)}) copy-start(s32[2]{0:T(128)} %given_10_.1) | copy-start | bytes 28
where the time goes:
time: 128 us; the launch traced here: 127 us
  Pallas kernels  125 us (98%)
  between operations  2.14 us (2%)
    pallas_call x1, Pallas kernels, run_block(): pl.pallas_call(functools.partial(block_kernel, names), out_shape=(pltpu.V...  112 us
    pallas_call x1, Pallas kernels, run_end(): pl.pallas_call(end_kernel, out_shape=(shape((5760, 640), F32), shape((576...  12.9 us

commit v1 on v0

--- a/solution.py
+++ b/solution.py
@@ -834,39 +834,40 @@
 
 TICKS = {
     6: (0,),
-    8: (6, 1,),
-    9: (2,),
-    10: (7,),
-    11: (12, 8,),
+    7: (1,),
+    8: (6, 2,),
+    9: (7,),
+    10: (8,),
+    11: (12,),
     12: (78,),
     13: (13, 3,),
-    14: (4, 18, 14, 9,),
-    15: (5, 19, 10, 84,),
-    17: (11, 20,),
-    19: (15, 85,),
-    21: (16, 25,),
-    22: (24,),
-    23: (17, 86,),
-    24: (26,),
-    25: (21, 30, 22,),
-    26: (31,),
-    27: (32, 23, 87,),
-    28: (36,),
-    29: (27,),
-    30: (28, 38,),
-    32: (29, 33,),
-    33: (34, 37, 42,),
-    34: (35, 39,),
-    35: (40,),
-    37: (44, 43, 41,),
-    39: (45, 46,),
-    41: (48, 47,),
-    42: (49,),
-    45: (50, 51,),
-    46: (52, 53, 54,),
-    47: (56, 55, 57,),
-    48: (62, 58, 60, 59,),
-    49: (66, 67, 68, 69, 70, 71, 72, 73, 74, 63, 64, 61, 65,),
+    14: (14, 4, 18, 9,),
+    15: (5, 19, 84,),
+    16: (10,),
+    17: (11, 15,),
+    18: (24,),
+    19: (25, 20, 85,),
+    21: (16,),
+    22: (21, 17,),
+    23: (86,),
+    24: (30, 26, 22, 31,),
+    26: (23, 32, 27,),
+    27: (37, 36, 87,),
+    28: (28, 38,),
+    30: (29, 33,),
+    31: (34,),
+    32: (42,),
+    33: (35, 39, 43,),
+    34: (40, 44,),
+    37: (41,),
+    38: (45, 46, 48,),
+    41: (47,),
+    43: (50,),
+    45: (49, 51,),
+    46: (52, 53,),
+    47: (54, 56, 55, 57,),
+    48: (58, 63, 61, 59,),
+    49: (66, 67, 68, 69, 70, 71, 72, 73, 74, 64, 60, 62, 65,),
 }
 
 B_INPUTS = INPUTS + (

time: 128 us -> 127 us (level)
  Pallas kernels: 125 us -> 123 us
where the time goes in v1:
time: 127 us; the launch traced here: 126 us
  Pallas kernels  123 us (97%)
  between operations  2.14 us (2%)
    pallas_call x1, Pallas kernels, run_block(): pl.pallas_call(functools.partial(block_kernel, names), out_shape=(pltpu.V...  111 us
    pallas_call x1, Pallas kernels, run_end(): pl.pallas_call(end_kernel, out_shape=(shape((5760, 640), F32), shape((576...  12.9 us

profile of v1, /device:TPU:6, one launch (start us, length us, event | category | flops | bytes accessed | tf_op | source)
XLA Modules:
  0.0 125.6 jit_solution(7282616119442186269)
XLA Ops:
  1.9 0.0 copy-start
  1.9 110.6 %shard_map.258 = (bf16[2,3,1920,640]{3,2,1,0:T(8,128)(2,1)S(1)}, bf16[16,8,640]{2,1,0:T(8,128)(2,1)S(1)}, bf16[12,12,640]{2,1,0:T(8,128)(2,1)S(1)}, bf16[144,4,6...) custom-call(bf16[144,4,640]{2,1,0:T(4,128)(2,1)} %bitcast.44, ...), custom_call_target="tpu_custom_call" | custom-call | flops 35999997952 | bytes 83886080 | tf_op jit(solution)/shard_map/pallas_call | solution.py:919
  112.5 0.0 copy-done
  112.5 12.9 %shard_map.259 = (f32[5760,640]{1,0:T(8,128)}, f32[5760,640]{1,0:T(8,128)}, bf16[16,8,640]{2,1,0:T(8,128)(2,1)}, bf16[12,12,640]{2,1,0:T(8,128)(2,1)}, bf16[144,...) custom-call(bf16[2,3,1920,640]{3,2,1,0:T(8,128)(2,1)S(1)} %get-tuple, ...), custom_call_target="tpu_custom_call" | custom-call | tf_op jit(solution)/shard_map/pallas_call | solution.py:1006
Async XLA Ops:
  1.9 110.6 %copy-start = (s32[2]{0:T(128)S(1)}, s32[2]{0:T(128)}, u32[]{:S(2)}) copy-start(s32[2]{0:T(128)} %given_10_.1) | copy-start | bytes 28
